TPU v7x, 768 devices: a whole 4x8x12 slice. The times are simulated.
768 devices in a mesh: seq: 16 (over y_lo, x, core), grp: 48 (over z, y_hi).
Axes of the slice: x: 4, y: 8 (y_hi: 4, y_lo: 2; y = y_hi * 2 + y_lo), z: 12, core: 2. Of those that a mesh axis runs over, the one named last changes fastest.
Arguments:
- tokens: bfloat16 [48, 2048, 1408], P('grp', 'seq'), may hold values from -6 to 6
- target_kv: bfloat16 [1408, 1408], P('seq'), may hold values from -0.15625 to 0.15625
- context_kv: bfloat16 [1408, 1408], P('seq'), may hold values from -0.15625 to 0.15625
- query_weight: bfloat16 [704, 1408], replicated, may hold values from -0.15625 to 0.15625
- pred_hidden: bfloat16 [48, 2048, 384], P('grp', 'seq'), may hold values from -6 to 6
- pred_weight: bfloat16 [48, 704, 384], P('grp'), may hold values from -0.3125 to 0.3125
- target_mask: int32 [48, 1024], P('grp', 'seq'), may hold values 0 or 1
- owners: int32 [48, 1024, 1], P('grp', 'seq'), may hold values from 0 to 47; in each aligned block of 64 rows (0 to 63, 64 to 127, ..., all dimensions but the last counted through in order) at most 2 rows name the same one
Outputs:
- new_kv: bfloat16 [1408, 1408], P('seq')
- targets: bfloat16 [48, 2048, 704], P('grp', 'seq')
- pred_grad: bfloat16 [48, 2048, 384], P('grp', 'seq')
Inputs may be any that keep to these rules, and one draw needn't show every extreme that they name: `owners`: among the 64 token pairs of one device no owner is named more than 2 times, a bound that some block reaches.
All inputs are finite; a program needn't handle non-finite values. No bound on the sum of `target_mask` on one device may be relied on, other than what follows from the above.
Results may differ from a plain program's by a relative error of at most 0.011.
Values may be sent and summed in bfloat16 or wider, within the bound.
A program may use at most 64 MiB of HBM per device.

v0:
```python
import math

import jax
import jax.numpy as jnp
from jax import lax
from jax.sharding import PartitionSpec as P

HEAD = 64
HEADS = 11


keep_rate = 0.9
epsilon = 1e-05


def layer_norm(values):
    center = values - jnp.mean(values, axis=-1, keepdims=True)
    variance = jnp.mean(center * center, axis=-1, keepdims=True)
    return center * lax.rsqrt(variance + epsilon)


def norm_backward(upstream, normed, inputs):
    center = inputs - jnp.mean(inputs, axis=-1, keepdims=True)
    variance = jnp.mean(center * center, axis=-1, keepdims=True)
    inverse = lax.rsqrt(variance + epsilon)
    upstream_mean = jnp.mean(upstream, axis=-1, keepdims=True)
    cross_mean = jnp.mean(upstream * normed, axis=-1, keepdims=True)
    return inverse * (upstream - upstream_mean - normed * cross_mean)


def owner_compute(received, expert_weight):
    received_targets, received_hidden = received
    groups = received_targets.shape[0]
    items = received_targets.shape[1]
    pred_size = expert_weight.shape[1]
    width = expert_weight.shape[0]
    inputs = received_hidden.reshape(-1, pred_size).astype(jnp.float32)
    normed = layer_norm(inputs)
    prediction = jnp.einsum(
        "tp,ap->ta", normed.astype(jnp.bfloat16), expert_weight, preferred_element_type=jnp.float32
    )
    residual = prediction - received_targets.reshape(-1, width).astype(jnp.float32)
    upstream = jnp.dot(
        residual.astype(jnp.bfloat16), expert_weight, preferred_element_type=jnp.float32
    )
    grad = norm_backward(upstream, normed, inputs).astype(jnp.bfloat16)
    return grad.reshape(groups, items, 2 * pred_size)


def shards(
    tokens, target_kv, context_kv, query_weight, pred_hidden, pred_weight, target_mask, owners
):
    new_kv = (
        keep_rate * target_kv.astype(jnp.float32)
        + (1.0 - keep_rate) * context_kv.astype(jnp.float32)
    ).astype(jnp.bfloat16)
    width = HEADS * HEAD
    scale = 1.0 / math.sqrt(HEAD)
    rows = tokens.shape[1]
    normed = layer_norm(tokens[0].astype(jnp.float32)).astype(jnp.bfloat16)
    queries = jnp.einsum(
        "td,ad->ta", normed, query_weight, preferred_element_type=jnp.float32
    ).astype(jnp.bfloat16)
    query_heads = queries.reshape(rows, HEADS, HEAD)
    own_kv = jnp.dot(
        normed,
        lax.all_gather(new_kv, "seq", axis=0, tiled=True),
        preferred_element_type=jnp.float32,
    ).astype(jnp.bfloat16)
    key_values = lax.all_gather(own_kv, "seq", axis=0, tiled=True)
    count = key_values.shape[0]
    keys = key_values[:, :width].reshape(count, HEADS, HEAD)
    values = key_values[:, width:].reshape(count, HEADS, HEAD)
    scores = (
        jnp.einsum("qhd,khd->hqk", query_heads, keys, preferred_element_type=jnp.float32) * scale
    )
    expo = jnp.exp(scores)
    added = jnp.einsum(
        "hqk,khd->qhd", expo.astype(jnp.bfloat16), values, preferred_element_type=jnp.float32
    )
    numerator = added.reshape(rows, width)
    denominator = jnp.sum(expo, axis=-1)
    attended = (numerator.reshape(rows, HEADS, HEAD) / denominator.T[:, :, None]).reshape(
        rows, width
    )
    targets = layer_norm(attended).astype(jnp.bfloat16)
    blocks = target_mask.shape[1]
    groups = lax.axis_size("grp")
    capacity = max(2, (blocks + groups - 1) // groups)
    pred_size = pred_hidden.shape[2]
    owner_ids = owners[0, :, 0]
    live = target_mask[0]
    chosen = (
        (owner_ids[:, None] == jnp.arange(groups, dtype=jnp.int32)[None, :]) & (live[:, None] == 1)
    ).astype(jnp.int32)
    earlier = jnp.cumsum(chosen, axis=0) - chosen
    position = jnp.sum(earlier * chosen, axis=1)
    slot_index = owner_ids * capacity + position
    dispatch = (
        (jnp.arange(groups * capacity, dtype=jnp.int32)[:, None] == slot_index[None, :])
        & (live[None, :] == 1)
    ).astype(jnp.bfloat16)
    send_targets = (
        jnp.dot(dispatch, targets.reshape(blocks, 2 * width), preferred_element_type=jnp.float32)
        .astype(jnp.bfloat16)
        .reshape(groups, capacity, 2 * width)
    )
    send_hidden = (
        jnp.dot(
            dispatch,
            pred_hidden[0].reshape(blocks, 2 * pred_size),
            preferred_element_type=jnp.float32,
        )
        .astype(jnp.bfloat16)
        .reshape(groups, capacity, 2 * pred_size)
    )
    expert_weight = pred_weight[0]
    owner_grads = owner_compute(
        (
            lax.all_to_all(send_targets, "grp", split_axis=0, concat_axis=0, tiled=True),
            lax.all_to_all(send_hidden, "grp", split_axis=0, concat_axis=0, tiled=True),
        ),
        expert_weight,
    )
    back_grads = lax.all_to_all(owner_grads, "grp", split_axis=0, concat_axis=0, tiled=True)
    pair_grads = jnp.dot(
        dispatch.T,
        back_grads.reshape(groups * capacity, 2 * pred_size),
        preferred_element_type=jnp.float32,
    )
    pred_grad = pair_grads.astype(jnp.bfloat16).reshape(rows, pred_size)
    return (new_kv, targets[None], pred_grad[None])


def solution(mesh):
    placed = (
        P("grp", "seq", None),
        P("seq", None),
        P("seq", None),
        P(),
        P("grp", "seq", None),
        P("grp", None, None),
        P("grp", "seq"),
        P("grp", "seq", None),
    )
    return jax.shard_map(
        shards,
        mesh=mesh,
        in_specs=placed,
        out_specs=(P("seq", None), P("grp", "seq", None), P("grp", "seq", None)),
        check_vma=False,
    )
```

profile of v0, /device:TPU:2, one launch (start us, length us, event | category | flops | bytes accessed | tf_op | source)
XLA Modules:
  0.0 217.6 jit_solution(10178473971578416823)
XLA Ops:
  7.3 2.0 add_convert_fusion
  9.3 1.1 convert_reduce_fusion
  10.5 1.2 fusion.16
  11.7 51.1 %all-gather.3.cloned.1.call-done = bf16[1408,1408]{1,0:T(8,128)(2,1)} async-done(((bf16[88,1408]{1,0:T(8,128)(2,1)}), bf16[1408,1408]{1,0:T(8,128)(2,1)}) %all-gather.3.cloned.1.call-update) | async-done | bytes 3964944 | tf_op jit(solution)/shard_map/all_gather | solution.py:67
  62.8 3.8 %convolution_convert_fusion = bf16[128,1408]{1,0:T(8,128)(2,1)} fusion(bf16[1408,1408]{1,0:T(8,128)(2,1)} %all-gather.3.cloned.1.call-done, bf16[1,128,1408]{2,1,0:T(8,128)(2,1)} %param.8, f32[128]{0:T(128)S(1)} %add_rsqrt_fusion.2, f32[128]{0:T(128)S(1)} %broadcast_multiply_fusion.4), kind=kOutput, calls=%fused_computation.5 | convolution fusion | flops 508411904 | bytes 4686848 | tf_op jit(solution)/shard_map/dot_general | solution.py:65
  68.0 15.1 %all-to-all-start = ((bf16[48,2,768]{2,1,0:T(2,128)(2,1)}), bf16[48,2,768]{2,1,0:T(2,128)(2,1)S(1)}, u32[]{:S(2)}, u32[]{:S(2)}) async-start(bf16[48,2,768]{2,1,0:T(2,128)(2,1)} %reshape.198), calls=%async_computation | async-start | bytes 294912 | tf_op jit(solution)/shard_map/all_to_all | solution.py:121
  83.9 16.4 %all-to-all-done = bf16[48,2,768]{2,1,0:T(2,128)(2,1)S(1)} async-done(((bf16[48,2,768]{2,1,0:T(2,128)(2,1)}), bf16[48,2,768]{2,1,0:T(2,128)(2,1)S(1)}, u32[]{:S(2)}, u32[]{:S(2)}) %all-to-all-start) | async-done | bytes 147488 | tf_op jit(solution)/shard_map/all_to_all | solution.py:121
  100.5 17.5 %all-gather.5.cloned.1.call-done = bf16[2048,1408]{1,0:T(8,128)(2,1)} async-done(((bf16[128,1408]{1,0:T(8,128)(2,1)}), bf16[2048,1408]{1,0:T(8,128)(2,1)}) %all-gather.5.cloned.1.call-update) | async-done | bytes 5767184 | tf_op jit(solution)/shard_map/all_gather | solution.py:70
  118.0 7.2 %fusion.38 = (bf16[2048,704]{1,0:T(8,128)(2,1)}, bf16[2048,704]{1,0:T(8,128)(2,1)}) fusion(bf16[2048,1408]{1,0:T(8,128)(2,1)} %all-gather.5.cloned.1.call-done), kind=kLoop, calls=%fused_computation.57 | loop fusion | bytes 11534336 | tf_op jit(solution)/shard_map/slice | solution.py:72
  125.2 4.7 %copy.14 = bf16[2048,704]{0,1:T(8,128)(2,1)} copy(bf16[2048,704]{1,0:T(8,128)(2,1)} %get-tuple-element.5) | data formatting | bytes 5767168 | tf_op jit(solution)/shard_map/slice | solution.py:72
  129.9 4.7 %copy.13 = bf16[2048,704]{0,1:T(8,128)(2,1)} copy(bf16[2048,704]{1,0:T(8,128)(2,1)} %get-tuple-element.6) | data formatting | bytes 5767168 | tf_op jit(solution)/shard_map/slice | solution.py:73
  134.6 3.9 %fusion = (f32[11,128]{1,0:T(8,128)S(1)}, f32[11,128,2048]{2,1,0:T(8,128)S(1)}) fusion(bf16[128,11,64]{0,2,1:T(8,128)(2,1)S(1)} %bitcast.50, bf16[2048,11,64]{0,2,1:T(8,128)(2,1)} %bitcast.49), kind=kOutput, calls=%fused_computation.1 | convolution fusion | flops 374864512 | bytes 14603776 | tf_op jit(solution)/shard_map/qhd,khd->hqk/dot_general | solution.py:75
  138.5 2.1 fusion.39
  140.6 1.4 copy.15
  143.9 2.3 %reshape.199 = f32[64,1408]{1,0:T(8,128)} reshape(f32[128,11,64]{2,1,0:T(8,128)} %copy.15) | data formatting | bytes 720896 | tf_op jit(solution)/shard_map/reshape | solution.py:83
  148.1 1.3 convolution_convert_fusion.1
  150.3 14.0 %all-to-all-start.1 = ((bf16[48,2,1408]{2,1,0:T(2,128)(2,1)}), bf16[48,2,1408]{2,1,0:T(2,128)(2,1)}, u32[]{:S(2)}, u32[]{:S(2)}) async-start(bf16[48,2,1408]{2,1,0:T(2,128)(2,1)} %reshape.200), calls=%async_computation.1 | async-start | bytes 540672 | tf_op jit(solution)/shard_map/all_to_all | solution.py:120
  166.3 1.3 sub.81
  168.5 16.2 %all-to-all-done.1 = bf16[48,2,1408]{2,1,0:T(2,128)(2,1)} async-done(((bf16[48,2,1408]{2,1,0:T(2,128)(2,1)}), bf16[48,2,1408]{2,1,0:T(2,128)(2,1)}, u32[]{:S(2)}, u32[]{:S(2)}) %all-to-all-start.1) | async-done | bytes 270368 | tf_op jit(solution)/shard_map/all_to_all | solution.py:120
  184.8 1.2 reshape.204
  186.0 2.0 fusion.37
  188.9 4.6 %all-to-all-start.2 = ((bf16[48,2,768]{2,1,0:T(2,128)(2,1)}), bf16[48,2,768]{2,1,0:T(2,128)(2,1)S(1)}, u32[]{:S(2)}, u32[]{:S(2)}) async-start(bf16[48,2,768]{2,1,0:T(2,128)(2,1)} %reshape.201), calls=%async_computation.2 | async-start | bytes 294912 | tf_op jit(solution)/shard_map/all_to_all | solution.py:125
  193.5 1.4 fusion.21
  194.9 14.9 %all-to-all-done.2 = bf16[48,2,768]{2,1,0:T(2,128)(2,1)S(1)} async-done(((bf16[48,2,768]{2,1,0:T(2,128)(2,1)}), bf16[48,2,768]{2,1,0:T(2,128)(2,1)S(1)}, u32[]{:S(2)}, u32[]{:S(2)}) %all-to-all-start.2) | async-done | bytes 147488 | tf_op jit(solution)/shard_map/all_to_all | solution.py:125
  (59 shorter events, 11.8 us)
Async XLA Ops:
  7.2 75.9 %copy-start = (bf16[704,1408]{1,0:T(8,128)(2,1)S(1)}, bf16[704,1408]{1,0:T(8,128)(2,1)}, u32[]{:S(2)}) copy-start(bf16[704,1408]{1,0:T(8,128)(2,1)} %param.11) | copy-start | bytes 5947396
  7.2 75.9 %copy-start.2 = (bf16[1,128,1408]{2,1,0:T(8,128)(2,1)S(1)}, bf16[1,128,1408]{2,1,0:T(8,128)(2,1)}, u32[]{:S(2)}) copy-start(bf16[1,128,1408]{2,1,0:T(8,128)(2,1)} %param.8) | copy-start | bytes 1081348
  7.2 59.5 %copy-start.3 = (bf16[1,128,384]{2,1,0:T(8,128)(2,1)S(1)}, bf16[1,128,384]{2,1,0:T(8,128)(2,1)}, u32[]{:S(2)}) copy-start(bf16[1,128,384]{2,1,0:T(8,128)(2,1)} %param.12) | copy-start | bytes 294916
  7.2 59.5 %copy-start.7 = (s32[1,64]{1,0:T(1,128)S(1)}, s32[1,64]{1,0:T(1,128)}, u32[]{:S(2)}) copy-start(s32[1,64]{1,0:T(1,128)} %param.14) | copy-start | bytes 772
  7.2 59.5 %copy-start.5 = (s32[1,64,1]{1,2,0:T(1,128)S(1)}, s32[1,64,1]{1,2,0:T(1,128)}, u32[]{:S(2)}) copy-start(s32[1,64,1]{1,2,0:T(1,128)} %param.15) | copy-start | bytes 772
  7.2 55.6 %all-gather.3.cloned.1.call-start = ((), (), s32[]{:S(2)}) async-start(), calls=%async_computation.3 | async-start | bytes 4212736 | tf_op jit(solution)/shard_map/all_gather | solution.py:67
  9.3 108.7 %all-gather.5.cloned.1.call-start = ((), (), s32[]{:S(2)}) async-start(), calls=%async_computation.4 | async-start | bytes 6127616 | tf_op jit(solution)/shard_map/all_gather | solution.py:70
  68.0 32.2 %all-to-all-start = ((bf16[48,2,768]{2,1,0:T(2,128)(2,1)}), bf16[48,2,768]{2,1,0:T(2,128)(2,1)S(1)}, u32[]{:S(2)}, u32[]{:S(2)}) async-start(bf16[48,2,768]{2,1,0:T(2,128)(2,1)} %reshape.198), calls=%async_computation | async-start | bytes 294912 | tf_op jit(solution)/shard_map/all_to_all | solution.py:121
  134.6 3.9 %copy-start.1 = (bf16[2048,704]{0,1:T(8,128)(2,1)S(1)}, bf16[2048,704]{0,1:T(8,128)(2,1)}, u32[]{:S(2)}) copy-start(bf16[2048,704]{0,1:T(8,128)(2,1)} %copy.13) | copy-start | bytes 8650756
  140.6 9.6 %copy-start.4 = (f32[128]{0:T(128)}, f32[128]{0:T(128)S(1)}, u32[]{:S(2)}) copy-start(f32[128]{0:T(128)S(1)} %broadcast_multiply_fusion.3) | copy-start | bytes 1540
  142.9 0.6 copy-start.6
  150.3 34.5 %all-to-all-start.1 = ((bf16[48,2,1408]{2,1,0:T(2,128)(2,1)}), bf16[48,2,1408]{2,1,0:T(2,128)(2,1)}, u32[]{:S(2)}, u32[]{:S(2)}) async-start(bf16[48,2,1408]{2,1,0:T(2,128)(2,1)} %reshape.200), calls=%async_computation.1 | async-start | bytes 540672 | tf_op jit(solution)/shard_map/all_to_all | solution.py:120
  188.9 20.9 %all-to-all-start.2 = ((bf16[48,2,768]{2,1,0:T(2,128)(2,1)}), bf16[48,2,768]{2,1,0:T(2,128)(2,1)S(1)}, u32[]{:S(2)}, u32[]{:S(2)}) async-start(bf16[48,2,768]{2,1,0:T(2,128)(2,1)} %reshape.201), calls=%async_computation.2 | async-start | bytes 294912 | tf_op jit(solution)/shard_map/all_to_all | solution.py:125
Sparse Core Ops, SparseCore 0:
  11.1 51.6 all-gather.2
  66.8 51.1 all-gather.4
where the time goes:
time: 218 us
  waiting for transfers between devices  116 us (53%)
  starting transfers between devices  33.8 us (16%)
  local copies, waits for them, and re-layouts  32.1 us (15%)
  matrix products  14.3 us (7%)
  between operations  14.3 us (7%)
  other arithmetic  6.93 us (3%)
    all_gather x1, waiting for transfers between devices, shards(): lax.all_gather(new_kv, 'seq', axis=0, tiled=True)  51.1 us
    all_gather x1, waiting for transfers between devices, shards(): key_values = lax.all_gather(own_kv, 'seq', axis=0, tiled=True)  17.5 us
    all_to_all x1, waiting for transfers between devices, shards(): lax.all_to_all(send_hidden, 'grp', split_axis=0, concat_axis=0, tiled=True)  16.4 us
    all_to_all x1, waiting for transfers between devices, shards(): lax.all_to_all(send_targets, 'grp', split_axis=0, concat_axis=0, tiled=True)  16.2 us
    all_to_all x1, starting transfers between devices, shards(): lax.all_to_all(send_hidden, 'grp', split_axis=0, concat_axis=0, tiled=True)  15.1 us
    all_to_all x1, waiting for transfers between devices, shards(): lax.all_to_all(owner_grads, 'grp', split_axis=0, concat_axis=0, tiled=True)  14.9 us
    all_to_all x1, starting transfers between devices, shards(): lax.all_to_all(send_targets, 'grp', split_axis=0, concat_axis=0, tiled=True)  14 us
    slice x2, local copies, waits for them, and re-layouts, shards(): keys = key_values[:, :width].reshape(count, HEADS, HEAD)  11.9 us
  transfers between devices with their start and end apart: 5, of which 5 were waited for; matrix products, arithmetic and copies ran while one was open for 5% of the time, Pallas kernels for 0%

commit v1 on v0

v1 whole, which is shorter than its diff:
```python
import math

import jax
import jax.numpy as jnp
from jax import lax
from jax.experimental import pallas as pl
from jax.experimental.pallas import tpu as pltpu
from jax.sharding import PartitionSpec as P

HEAD = 64
HEADS = 11
SEQ = 16
GRP = 48
ROWS = 128
PAIRS = 64
D = 1408
ATT = 704
PRED = 384
SHARD = 88
LO = 768
SLAB = 4
SLOTS = GRP * SLAB

keep_rate = 0.9
epsilon = 1e-05

F32 = jnp.float32
BF16 = jnp.bfloat16


def normalize(values):
    center = values - jnp.mean(values, axis=-1, keepdims=True)
    variance = jnp.mean(center * center, axis=-1, keepdims=True)
    inverse = lax.rsqrt(variance + epsilon)
    return center * inverse, inverse


def dot(a, b):
    return jnp.dot(a, b, preferred_element_type=F32)


def dot_t(a, b):
    return lax.dot_general(a, b, (((1,), (1,)), ((), ())), preferred_element_type=F32)


def iota(shape, axis):
    return lax.broadcasted_iota(jnp.int32, shape, axis)


def slot_rows(own_col, mask_row):
    shape = (PAIRS, PAIRS)
    down, across = iota(shape, 0), iota(shape, 1)
    same = down == across
    own_down = jnp.broadcast_to(own_col, shape)
    live_across = jnp.broadcast_to(mask_row, shape)
    own_across = jnp.broadcast_to(
        jnp.sum(jnp.where(same, own_down, 0.0), axis=0, keepdims=True), shape
    )
    live_down = jnp.broadcast_to(
        jnp.sum(jnp.where(same, live_across, 0.0), axis=1, keepdims=True), shape
    )
    equal = own_down == own_across
    rank_row = jnp.sum(
        jnp.where(equal & (down < across), live_down, 0.0), axis=0, keepdims=True
    )
    rank_col = jnp.sum(
        jnp.where(equal & (across < down), live_across, 0.0), axis=1, keepdims=True
    )
    slot_row = jnp.where(mask_row > 0.5, own_across[:1] * 2.0 + rank_row, -1.0)
    slot_col = jnp.where(live_down[:, :1] > 0.5, own_col * 2.0 + rank_col, -1.0)
    shape = (PAIRS, ROWS)
    token_row = jnp.sum(
        jnp.where(
            iota(shape, 0) == lax.shift_right_logical(iota(shape, 1), 1),
            jnp.broadcast_to(slot_col, shape),
            0.0,
        ),
        axis=0,
        keepdims=True,
    )
    shape = (ROWS, PAIRS)
    token_col = jnp.sum(
        jnp.where(
            lax.shift_right_logical(iota(shape, 0), 1) == iota(shape, 1),
            jnp.broadcast_to(slot_row, shape),
            0.0,
        ),
        axis=1,
        keepdims=True,
    )
    return token_row, token_col


def kernel(
    tok_ref,
    tkv_ref,
    ckv_ref,
    qw_ref,
    hid_ref,
    pw_ref,
    mask_ref,
    own_ref,
    nkv_ref,
    tgt_ref,
    pg_ref,
    wbuf,
    chunks,
    acc,
    queries,
    head_out,
    head_in,
    values_one,
    att_out,
    att_in,
    spread,
    gather,
    hid_out,
    hid_in,
    tgt_out,
    tgt_in,
    grad_out,
    grad_in,
    predicted,
    w_send,
    w_recv,
    head_send,
    head_recv,
    att_send,
    att_recv,
    hid_send,
    hid_recv,
    tgt_send,
    tgt_recv,
    grad_send,
    grad_recv,
):
    me = lax.axis_index("seq")
    mine = lax.axis_index("grp")
    core = lax.rem(me, 2)
    x = lax.rem(me // 2, 4)
    y = me // 8
    z = mine // 4
    yh = lax.rem(mine, 4)

    def place(xx, yy, cc):
        return (lax.rem(xx, 4) + yy * 4) * 2 + cc

    right, left, far = place(x + 1, y, core), place(x + 3, y, core), place(x + 2, y, core)
    across = place(x, 1 - y, core)
    right_p, left_p, far_p = (
        place(x + 1, 1 - y, core),
        place(x + 3, 1 - y, core),
        place(x + 2, 1 - y, core),
    )
    twin = place(x, y, 1 - core)
    up_grp = z * 4 + lax.rem(yh + y, 4)
    down_grp = z * 4 + lax.rem(yh + 3 * (1 - y), 4)
    other_grp = z * 4 + lax.rem(yh + 3 + 2 * y, 4)

    barrier = pltpu.get_barrier_semaphore()

    @pl.loop(1, SEQ)
    def _(k):
        pl.semaphore_signal(barrier, inc=1, device_id={"seq": lax.rem(me + k, SEQ), "grp": mine})

    @pl.loop(1, GRP)
    def _(k):
        pl.semaphore_signal(barrier, inc=1, device_id={"seq": me, "grp": lax.rem(mine + k, GRP)})

    pl.semaphore_signal(barrier, inc=1, device_id={"seq": across, "grp": other_grp})

    blended = (
        keep_rate * tkv_ref[...].astype(F32) + (1.0 - keep_rate) * ckv_ref[...].astype(F32)
    ).astype(BF16)
    nkv_ref[...] = blended
    wbuf[me] = blended
    pl.semaphore_wait(barrier, SEQ - 1 + GRP - 1 + 1)

    started = []

    def push(ref, slot, seq, grp):
        copy = pltpu.make_async_remote_copy(
            src_ref=ref,
            dst_ref=ref,
            send_sem=w_send.at[len(started)],
            recv_sem=w_recv.at[slot],
            device_id={"seq": seq, "grp": grp},
        )
        copy.start()
        started.append(copy)

    def arrive(ref, slot):
        pltpu.make_async_remote_copy(
            src_ref=ref,
            dst_ref=ref,
            send_sem=w_send.at[0],
            recv_sem=w_recv.at[slot],
            device_id={"seq": twin, "grp": mine},
        ).wait_recv()

    def lo(block):
        return wbuf.at[block, :, pl.ds(0, LO)]

    def hi(block):
        return wbuf.at[block, :, pl.ds(LO, D - LO)]

    push(wbuf.at[me], 0, right, mine)
    push(wbuf.at[me], 1, left, mine)
    push(lo(me), 2, across, up_grp)
    push(hi(me), 3, across, down_grp)
    push(wbuf.at[me], 10, twin, mine)

    normed = normalize(tok_ref[...].astype(F32))[0]
    for s in range(SEQ):
        chunks[s] = normed[:, s * SHARD : (s + 1) * SHARD].astype(BF16)
    queries[...] = dot_t(normed.astype(BF16), qw_ref[...])
    token_row, token_col = slot_rows(
        own_ref[...].astype(F32), mask_ref[...].astype(F32)
    )
    shape = (SLOTS, ROWS)
    spread[...] = jnp.where(
        (
            lax.shift_right_logical(iota(shape, 0), 1)
            == jnp.broadcast_to(token_row, shape).astype(jnp.int32)
        )
        & (lax.bitwise_and(iota(shape, 0), 1) == lax.bitwise_and(iota(shape, 1), 1)),
        1.0,
        0.0,
    ).astype(BF16)
    shape = (ROWS, SLOTS)
    gather[...] = jnp.where(
        (
            lax.shift_right_logical(iota(shape, 1), 1)
            == jnp.broadcast_to(token_col, shape).astype(jnp.int32)
        )
        & (lax.bitwise_and(iota(shape, 0), 1) == lax.bitwise_and(iota(shape, 1), 1)),
        1.0,
        0.0,
    ).astype(BF16)

    def to_slabs(rows, out):
        out[...] = rows.reshape(GRP, SLAB, rows.shape[1]).astype(BF16)

    to_slabs(dot(spread[...], hid_ref[...]), hid_out)

    def term(block):
        return dot(chunks[block], wbuf[block])

    acc[...] = term(me)
    arrive(wbuf.at[left], 0)
    push(lo(left), 4, right, mine)
    push(wbuf.at[left], 6, across, up_grp)
    push(wbuf.at[left], 11, twin, mine)
    arrive(wbuf.at[right], 1)
    push(hi(right), 5, left, mine)
    push(wbuf.at[right], 7, across, down_grp)
    push(wbuf.at[right], 12, twin, mine)
    arrive(lo(across), 2)
    arrive(hi(across), 3)
    push(wbuf.at[across], 13, twin, mine)
    twin_of = 1 - 2 * core
    arrive(wbuf.at[twin], 10)
    acc[...] += term(left) + term(right)
    acc[...] += term(across) + term(twin)
    arrive(lo(far), 4)
    push(lo(far), 8, across, up_grp)
    arrive(hi(far), 5)
    push(hi(far), 9, across, down_grp)
    push(wbuf.at[far], 14, twin, mine)
    arrive(wbuf.at[left + twin_of], 11)
    arrive(wbuf.at[right + twin_of], 12)
    arrive(wbuf.at[across + twin_of], 13)
    acc[...] += term(far) + term(left + twin_of)
    acc[...] += term(right + twin_of) + term(across + twin_of)
    arrive(wbuf.at[left_p], 6)
    push(wbuf.at[left_p], 15, twin, mine)
    arrive(wbuf.at[right_p], 7)
    push(wbuf.at[right_p], 16, twin, mine)
    arrive(wbuf.at[far + twin_of], 14)
    acc[...] += term(left_p) + term(right_p) + term(far + twin_of)
    arrive(lo(far_p), 8)
    arrive(hi(far_p), 9)
    push(wbuf.at[far_p], 17, twin, mine)
    acc[...] += term(far_p)
    arrive(wbuf.at[left_p + twin_of], 15)
    arrive(wbuf.at[right_p + twin_of], 16)
    acc[...] += term(left_p + twin_of) + term(right_p + twin_of)
    arrive(wbuf.at[far_p + twin_of], 17)
    acc[...] += term(far_p + twin_of)

    def head_place(h):
        return 2 * h if h < 8 else 1 + 4 * (h - 8)

    for h in range(HEADS):
        k_h = acc[:, h * HEAD : (h + 1) * HEAD]
        v_h = acc[:, ATT + h * HEAD : ATT + (h + 1) * HEAD]
        q_h = queries[:, h * HEAD : (h + 1) * HEAD]
        head_out[h, :ROWS] = jnp.concatenate([v_h, k_h], axis=1).astype(BF16)
        head_out[h, ROWS:] = jnp.concatenate([q_h[PAIRS:], q_h[:PAIRS]], axis=1).astype(BF16)
        to = head_place(h)

        @pl.when(me != to)
        def _():
            pltpu.make_async_remote_copy(
                src_ref=head_out.at[h],
                dst_ref=head_in.at[me],
                send_sem=head_send.at[h],
                recv_sem=head_recv.at[me],
                device_id={"seq": to, "grp": mine},
            ).start()

        @pl.when(me == to)
        def _():
            pltpu.make_async_copy(head_out.at[h], head_in.at[me], head_recv.at[me]).start()

    def exchange(out, into, send, recv):
        @pl.loop(1, GRP)
        def _(k):
            to = lax.rem(mine + k, GRP)
            pltpu.make_async_remote_copy(
                src_ref=out.at[to],
                dst_ref=into.at[mine],
                send_sem=send.at[to],
                recv_sem=recv.at[mine],
                device_id={"seq": me, "grp": to},
            ).start()

        pltpu.make_async_copy(out.at[mine], into.at[mine], recv.at[mine]).start()

    def received(out, into, send, recv):
        @pl.loop(0, GRP)
        def _(k):
            pltpu.make_async_copy(out.at[k], into.at[k], recv.at[k]).wait()

    def sent(out, into, send, recv):
        @pl.loop(1, GRP)
        def _(k):
            to = lax.rem(mine + k, GRP)
            pltpu.make_async_copy(out.at[to], into.at[to], send.at[to]).wait()

    hid_way = (hid_out, hid_in, hid_send, hid_recv)
    tgt_way = (tgt_out, tgt_in, tgt_send, tgt_recv)
    grad_way = (grad_out, grad_in, grad_send, grad_recv)
    exchange(*hid_way)

    even = lax.rem(me, 2) == 0
    is_head = even | ((lax.rem(me, 4) == 1) & (me < 12))
    my_head = jnp.where(even, me // 2, 8 + me // 4)

    @pl.when(is_head)
    def _():
        @pl.loop(0, SEQ)
        def _(t):
            pltpu.make_async_copy(head_out.at[0], head_in.at[t], head_recv.at[t]).wait()

        lane = iota((ROWS, 2 * HEAD), 1)

        @pl.loop(0, SEQ)
        def _(t):
            block = head_in[t, :ROWS].astype(F32)
            values_one[t] = jnp.where(lane < HEAD, block, 1.0).astype(BF16)

        rate = math.log2(math.e) / math.sqrt(HEAD)

        @pl.loop(0, SEQ // 2)
        def _(i):
            zero = jnp.zeros((PAIRS, HEAD), BF16)
            parts = []
            for j in range(2):
                packed = head_in[2 * i + j, ROWS:]
                parts.append(jnp.concatenate([zero, packed[:, HEAD:]], axis=1))
                parts.append(jnp.concatenate([zero, packed[:, :HEAD]], axis=1))
            q = jnp.concatenate(parts, axis=0)
            kv = head_in[:, :ROWS].reshape(SEQ * ROWS, 2 * HEAD)
            score = dot_t(q, kv)
            expo = jnp.exp2(score * rate).astype(BF16)
            added = dot(expo, values_one[...].reshape(SEQ * ROWS, 2 * HEAD))
            attended = added[:, :HEAD] / added[:, HEAD:]
            for j in range(2):
                rows = attended[j * ROWS : (j + 1) * ROWS]
                to = 2 * i + j
                att_out[to] = jnp.concatenate([rows[:PAIRS], rows[PAIRS:]], axis=1).astype(BF16)

                @pl.when(me != to)
                def _():
                    pltpu.make_async_remote_copy(
                        src_ref=att_out.at[to],
                        dst_ref=att_in.at[my_head],
                        send_sem=att_send.at[to],
                        recv_sem=att_recv.at[my_head],
                        device_id={"seq": to, "grp": mine},
                    ).start()

                @pl.when(me == to)
                def _():
                    pltpu.make_async_copy(
                        att_out.at[to], att_in.at[my_head], att_recv.at[my_head]
                    ).start()

    @pl.loop(0, HEADS)
    def _(h):
        pltpu.make_async_copy(att_out.at[0], att_in.at[h], att_recv.at[h]).wait()

    top = jnp.concatenate([att_in[h][:, :HEAD].astype(F32) for h in range(HEADS)], axis=1)
    low = jnp.concatenate([att_in[h][:, HEAD:].astype(F32) for h in range(HEADS)], axis=1)
    attended = jnp.concatenate([top, low], axis=0)
    targets = normalize(attended)[0].astype(BF16)
    tgt_ref[...] = targets
    to_slabs(dot(spread[...], targets), tgt_out)
    exchange(*tgt_way)

    def from_slabs(into):
        return into[...].reshape(SLOTS, into.shape[2])

    received(*hid_way)
    inputs = from_slabs(hid_in).astype(F32)
    normed_h, inverse = normalize(inputs)
    predicted[...] = dot_t(normed_h.astype(BF16), pw_ref[...])
    received(*tgt_way)
    residual = (predicted[...] - from_slabs(tgt_in).astype(F32)).astype(BF16)
    upstream = dot(residual, pw_ref[...])
    upstream_mean = jnp.mean(upstream, axis=-1, keepdims=True)
    cross_mean = jnp.mean(upstream * normed_h, axis=-1, keepdims=True)
    to_slabs(inverse * (upstream - upstream_mean - normed_h * cross_mean), grad_out)
    exchange(*grad_way)
    received(*grad_way)
    pg_ref[...] = dot(gather[...], from_slabs(grad_in)).astype(BF16)

    for copy in started:
        copy.wait_send()
    for h in range(HEADS):

        @pl.when(me != head_place(h))
        def _():
            pltpu.make_async_copy(head_out.at[h], head_in.at[0], head_send.at[h]).wait()

    @pl.when(is_head)
    def _():
        @pl.loop(1, SEQ)
        def _(k):
            to = lax.rem(me + k, SEQ)
            pltpu.make_async_copy(att_out.at[to], att_in.at[0], att_send.at[to]).wait()

    sent(*hid_way)
    sent(*tgt_way)
    sent(*grad_way)


def shards(
    tokens, target_kv, context_kv, query_weight, pred_hidden, pred_weight, target_mask, owners
):
    vmem = pl.BlockSpec(memory_space=pltpu.VMEM)
    dma = pltpu.SemaphoreType.DMA
    new_kv, targets, pred_grad = pl.pallas_call(
        kernel,
        out_shape=(
            jax.ShapeDtypeStruct((SHARD, D), BF16),
            jax.ShapeDtypeStruct((ROWS, ATT), BF16),
            jax.ShapeDtypeStruct((ROWS, PRED), BF16),
        ),
        in_specs=[vmem] * 8,
        out_specs=(vmem,) * 3,
        scratch_shapes=[
            pltpu.VMEM((SEQ, SHARD, D), BF16),
            pltpu.VMEM((SEQ, ROWS, SHARD), BF16),
            pltpu.VMEM((ROWS, D), F32),
            pltpu.VMEM((ROWS, ATT), F32),
            pltpu.VMEM((HEADS, ROWS + PAIRS, 2 * HEAD), BF16),
            pltpu.VMEM((SEQ, ROWS + PAIRS, 2 * HEAD), BF16),
            pltpu.VMEM((SEQ, ROWS, 2 * HEAD), BF16),
            pltpu.VMEM((SEQ, PAIRS, 2 * HEAD), BF16),
            pltpu.VMEM((HEADS, PAIRS, 2 * HEAD), BF16),
            pltpu.VMEM((SLOTS, ROWS), BF16),
            pltpu.VMEM((ROWS, SLOTS), BF16),
            pltpu.VMEM((GRP, SLAB, PRED), BF16),
            pltpu.VMEM((GRP, SLAB, PRED), BF16),
            pltpu.VMEM((GRP, SLAB, ATT), BF16),
            pltpu.VMEM((GRP, SLAB, ATT), BF16),
            pltpu.VMEM((GRP, SLAB, PRED), BF16),
            pltpu.VMEM((GRP, SLAB, PRED), BF16),
            pltpu.VMEM((SLOTS, ATT), F32),
            dma((24,)),
            dma((18,)),
            dma((HEADS,)),
            dma((SEQ,)),
            dma((SEQ,)),
            dma((HEADS,)),
            dma((GRP,)),
            dma((GRP,)),
            dma((GRP,)),
            dma((GRP,)),
            dma((GRP,)),
            dma((GRP,)),
        ],
        compiler_params=pltpu.CompilerParams(
            collective_id=0, has_side_effects=True, vmem_limit_bytes=48 * 1024 * 1024
        ),
        cost_estimate=pl.CostEstimate(
            flops=2_000_000_000, bytes_accessed=5_000_000, transcendentals=3_000_000
        ),
        name="attend_and_route",
    )(
        tokens[0],
        target_kv,
        context_kv,
        query_weight,
        pred_hidden[0],
        pred_weight[0],
        target_mask,
        owners[0],
    )
    return new_kv, targets[None], pred_grad[None]


def solution(mesh):
    placed = (
        P("grp", "seq", None),
        P("seq", None),
        P("seq", None),
        P(),
        P("grp", "seq", None),
        P("grp", None, None),
        P("grp", "seq"),
        P("grp", "seq", None),
    )
    return jax.shard_map(
        shards,
        mesh=mesh,
        in_specs=placed,
        out_specs=(P("seq", None), P("grp", "seq", None), P("grp", "seq", None)),
        check_vma=False,
    )
```

time: 218 us -> 106 us (0.49)
  the two profiles are of different devices: /device:TPU:2 before, /device:TPU:8 now
where the time goes in v1:
time: 106 us
  Pallas kernels  95.1 us (90%)
  local copies, waits for them, and re-layouts  9.9 us (9%)
    pallas_call x1, Pallas kernels, shards(): pl.pallas_call(kernel, out_shape=(jax.ShapeDtypeStruct((SHARD, D), BF16),...  95.1 us
    unnamed x17, local copies, waits for them, and re-layouts  9.16 us

profile of v1, /device:TPU:8, one launch (start us, length us, event | category | flops | bytes accessed | tf_op | source)
XLA Modules:
  0.0 105.7 jit_solution(15783557295912379189)
XLA Ops:
  0.6 0.7 copy.11.own_ref
  1.4 0.0 copy-start
  1.4 1.5 %copy-done = bf16[704,1408]{1,0:T(8,128)(2,1)S(1)} copy-done((bf16[704,1408]{1,0:T(8,128)(2,1)S(1)}, bf16[704,1408]{1,0:T(8,128)(2,1)}, u32[]{:S(2)}) %copy-start) | copy-done | bytes 1982488
  2.9 0.0 copy-start.1
  2.9 1.0 copy-done.1
  4.0 0.0 copy-start.2
  4.0 1.0 copy-done.2
  5.0 0.0 copy-start.3
  5.0 0.9 copy-done.3
  5.9 0.0 copy-start.4
  5.9 0.9 copy-done.4
  6.8 0.0 copy-start.5
  6.9 0.9 copy-done.5
  7.7 0.0 copy-start.6
  7.7 0.7 copy-done.6
  8.4 95.1 %attend_and_route.1 = (bf16[88,1408]{1,0:T(8,128)(2,1)S(1)}, bf16[128,704]{1,0:T(8,128)(2,1)S(1)}, bf16[128,384]{1,0:T(8,128)(2,1)S(1)}) custom-call(bf16[128,1408]{1,0:T(8,128)(2,1)S(1)} %bitcast.9, bf16[88,1408]{1,0:T(8,128)(2,1)S(1)} %copy-done.3, bf16[88,1408]{1,0:T(8,128)(2,1)S(1)} %copy-done.4, bf16[704,1408]{1,0:T(8,128)(2,1)S(1)} %copy-done, ...), custom_call_target="tpu_custom_call" | custom-call | flops 2000000000 | bytes 5000000 | tf_op jit(solution)/shard_map/attend_and_route/pallas_call | solution.py:454
  103.5 0.8 copy.12
  104.3 0.7 copy.15
  105.0 0.6 copy.16
Async XLA Ops:
  1.4 1.6 %copy-start = (bf16[704,1408]{1,0:T(8,128)(2,1)S(1)}, bf16[704,1408]{1,0:T(8,128)(2,1)}, u32[]{:S(2)}) copy-start(bf16[704,1408]{1,0:T(8,128)(2,1)} %qw_ref.1) | copy-start | bytes 5947396
  2.9 1.0 copy-start.1
  4.0 1.0 copy-start.2
  5.0 0.9 copy-start.3
  5.9 0.9 copy-start.4
  6.8 0.9 copy-start.5
  7.7 0.7 copy-start.6

commit v2 on v1

--- a/solution.py
+++ b/solution.py
@@ -47,18 +47,19 @@
     return lax.broadcasted_iota(jnp.int32, shape, axis)
 
 
-def slot_rows(own_col, mask_row):
+def slot_rows(own_row, mask_row):
     shape = (PAIRS, PAIRS)
     down, across = iota(shape, 0), iota(shape, 1)
     same = down == across
-    own_down = jnp.broadcast_to(own_col, shape)
+
+    def turned(row):
+        return jnp.broadcast_to(
+            jnp.sum(jnp.where(same, row, 0.0), axis=1, keepdims=True), shape
+        )
+
+    own_across = jnp.broadcast_to(own_row, shape)
     live_across = jnp.broadcast_to(mask_row, shape)
-    own_across = jnp.broadcast_to(
-        jnp.sum(jnp.where(same, own_down, 0.0), axis=0, keepdims=True), shape
-    )
-    live_down = jnp.broadcast_to(
-        jnp.sum(jnp.where(same, live_across, 0.0), axis=1, keepdims=True), shape
-    )
+    own_down, live_down = turned(own_across), turned(live_across)
     equal = own_down == own_across
     rank_row = jnp.sum(
         jnp.where(equal & (down < across), live_down, 0.0), axis=0, keepdims=True
@@ -67,7 +68,7 @@
         jnp.where(equal & (across < down), live_across, 0.0), axis=1, keepdims=True
     )
     slot_row = jnp.where(mask_row > 0.5, own_across[:1] * 2.0 + rank_row, -1.0)
-    slot_col = jnp.where(live_down[:, :1] > 0.5, own_col * 2.0 + rank_col, -1.0)
+    slot_col = jnp.where(live_down[:, :1] > 0.5, own_down[:, :1] * 2.0 + rank_col, -1.0)
     shape = (PAIRS, ROWS)
     token_row = jnp.sum(
         jnp.where(
@@ -91,7 +92,43 @@
     return token_row, token_col
 
 
+def dispatch_tables(own_row, mask_row):
+    token_row, token_col = slot_rows(own_row, mask_row)
+    shape = (SLOTS, ROWS)
+    spread = jnp.where(
+        (
+            lax.shift_right_logical(iota(shape, 0), 1)
+            == jnp.broadcast_to(token_row, shape).astype(jnp.int32)
+        )
+        & (lax.bitwise_and(iota(shape, 0), 1) == lax.bitwise_and(iota(shape, 1), 1)),
+        1.0,
+        0.0,
+    ).astype(BF16)
+    shape = (ROWS, SLOTS)
+    gather = jnp.where(
+        (
+            lax.shift_right_logical(iota(shape, 1), 1)
+            == jnp.broadcast_to(token_col, shape).astype(jnp.int32)
+        )
+        & (lax.bitwise_and(iota(shape, 0), 1) == lax.bitwise_and(iota(shape, 1), 1)),
+        1.0,
+        0.0,
+    ).astype(BF16)
+    return spread, gather
+
+
 def kernel(
+    tok_hbm,
+    tkv_hbm,
+    ckv_hbm,
+    qw_hbm,
+    hid_hbm,
+    pw_hbm,
+    mask_hbm,
+    own_hbm,
+    nkv_ref,
+    tgt_ref,
+    pg_ref,
     tok_ref,
     tkv_ref,
     ckv_ref,
@@ -100,9 +137,7 @@
     pw_ref,
     mask_ref,
     own_ref,
-    nkv_ref,
-    tgt_ref,
-    pg_ref,
+    load_sem,
     wbuf,
     chunks,
     acc,
@@ -121,6 +156,8 @@
     grad_out,
     grad_in,
     predicted,
+    normed_h,
+    inverses,
     w_send,
     w_recv,
     head_send,
@@ -134,6 +171,23 @@
     grad_send,
     grad_recv,
 ):
+    loads = [
+        pltpu.make_async_copy(src, dst, load_sem.at[i])
+        for i, (src, dst) in enumerate(
+            (
+                (tkv_hbm, tkv_ref),
+                (ckv_hbm, ckv_ref),
+                (tok_hbm, tok_ref),
+                (qw_hbm, qw_ref),
+                (mask_hbm, mask_ref),
+                (own_hbm, own_ref),
+                (hid_hbm, hid_ref),
+                (pw_hbm, pw_ref),
+            )
+        )
+    ]
+    for load in loads:
+        load.start()
     me = lax.axis_index("seq")
     mine = lax.axis_index("grp")
     core = lax.rem(me, 2)
@@ -169,6 +223,8 @@
 
     pl.semaphore_signal(barrier, inc=1, device_id={"seq": across, "grp": other_grp})
 
+    loads[0].wait()
+    loads[1].wait()
     blended = (
         keep_rate * tkv_ref[...].astype(F32) + (1.0 - keep_rate) * ckv_ref[...].astype(F32)
     ).astype(BF16)
@@ -204,88 +260,81 @@
     def hi(block):
         return wbuf.at[block, :, pl.ds(LO, D - LO)]
 
-    push(wbuf.at[me], 0, right, mine)
-    push(wbuf.at[me], 1, left, mine)
-    push(lo(me), 2, across, up_grp)
-    push(hi(me), 3, across, down_grp)
-    push(wbuf.at[me], 10, twin, mine)
-
+    push(lo(me), 0, right, mine)
+    push(hi(me), 3, left, mine)
+    push(lo(me), 4, across, up_grp)
+    push(hi(me), 5, across, down_grp)
+    push(hi(me), 1, right, mine)
+    push(lo(me), 2, left, mine)
+    push(wbuf.at[me], 14, twin, mine)
+
+    loads[2].wait()
     normed = normalize(tok_ref[...].astype(F32))[0]
     for s in range(SEQ):
         chunks[s] = normed[:, s * SHARD : (s + 1) * SHARD].astype(BF16)
-    queries[...] = dot_t(normed.astype(BF16), qw_ref[...])
-    token_row, token_col = slot_rows(
-        own_ref[...].astype(F32), mask_ref[...].astype(F32)
-    )
-    shape = (SLOTS, ROWS)
-    spread[...] = jnp.where(
-        (
-            lax.shift_right_logical(iota(shape, 0), 1)
-            == jnp.broadcast_to(token_row, shape).astype(jnp.int32)
-        )
-        & (lax.bitwise_and(iota(shape, 0), 1) == lax.bitwise_and(iota(shape, 1), 1)),
-        1.0,
-        0.0,
-    ).astype(BF16)
-    shape = (ROWS, SLOTS)
-    gather[...] = jnp.where(
-        (
-            lax.shift_right_logical(iota(shape, 1), 1)
-            == jnp.broadcast_to(token_col, shape).astype(jnp.int32)
-        )
-        & (lax.bitwise_and(iota(shape, 0), 1) == lax.bitwise_and(iota(shape, 1), 1)),
-        1.0,
-        0.0,
-    ).astype(BF16)
-
-    def to_slabs(rows, out):
-        out[...] = rows.reshape(GRP, SLAB, rows.shape[1]).astype(BF16)
-
-    to_slabs(dot(spread[...], hid_ref[...]), hid_out)
+    normed_b = normed.astype(BF16)
+    twin_of = 1 - 2 * core
 
     def term(block):
         return dot(chunks[block], wbuf[block])
 
-    acc[...] = term(me)
-    arrive(wbuf.at[left], 0)
-    push(lo(left), 4, right, mine)
-    push(wbuf.at[left], 6, across, up_grp)
-    push(wbuf.at[left], 11, twin, mine)
-    arrive(wbuf.at[right], 1)
-    push(hi(right), 5, left, mine)
-    push(wbuf.at[right], 7, across, down_grp)
-    push(wbuf.at[right], 12, twin, mine)
-    arrive(lo(across), 2)
-    arrive(hi(across), 3)
-    push(wbuf.at[across], 13, twin, mine)
-    twin_of = 1 - 2 * core
-    arrive(wbuf.at[twin], 10)
+    arrive(lo(left), 0)
+    push(lo(left), 6, right, mine)
+    push(lo(left), 8, across, up_grp)
+    arrive(hi(right), 3)
+    push(hi(right), 7, left, mine)
+    push(hi(right), 11, across, down_grp)
+    arrive(lo(across), 4)
+    arrive(hi(across), 5)
+    push(wbuf.at[across], 17, twin, mine)
+    loads[3].wait()
+    queries[...] = dot_t(normed_b, qw_ref[...])
+    arrive(hi(left), 1)
+    push(hi(left), 9, across, up_grp)
+    push(wbuf.at[left], 15, twin, mine)
+    arrive(lo(right), 2)
+    push(lo(right), 10, across, down_grp)
+    push(wbuf.at[right], 16, twin, mine)
+    arrive(wbuf.at[twin], 14)
+    acc[...] = term(me) + term(twin) + term(across)
+    arrive(lo(left_p), 8)
+    push(lo(left_p), 12, right, mine)
+    arrive(hi(right_p), 11)
+    push(hi(right_p), 13, left, mine)
     acc[...] += term(left) + term(right)
-    acc[...] += term(across) + term(twin)
-    arrive(lo(far), 4)
-    push(lo(far), 8, across, up_grp)
-    arrive(hi(far), 5)
-    push(hi(far), 9, across, down_grp)
-    push(wbuf.at[far], 14, twin, mine)
-    arrive(wbuf.at[left + twin_of], 11)
-    arrive(wbuf.at[right + twin_of], 12)
-    arrive(wbuf.at[across + twin_of], 13)
-    acc[...] += term(far) + term(left + twin_of)
-    acc[...] += term(right + twin_of) + term(across + twin_of)
-    arrive(wbuf.at[left_p], 6)
-    push(wbuf.at[left_p], 15, twin, mine)
-    arrive(wbuf.at[right_p], 7)
-    push(wbuf.at[right_p], 16, twin, mine)
-    arrive(wbuf.at[far + twin_of], 14)
+    arrive(lo(far), 6)
+    arrive(hi(far), 7)
+    push(wbuf.at[far], 18, twin, mine)
+    arrive(wbuf.at[left + twin_of], 15)
+    arrive(wbuf.at[right + twin_of], 16)
+    arrive(wbuf.at[across + twin_of], 17)
+    acc[...] += term(far) + term(left + twin_of) + term(right + twin_of) + term(across + twin_of)
+    arrive(hi(left_p), 9)
+    push(wbuf.at[left_p], 19, twin, mine)
+    arrive(lo(right_p), 10)
+    push(wbuf.at[right_p], 20, twin, mine)
+    arrive(wbuf.at[far + twin_of], 18)
     acc[...] += term(left_p) + term(right_p) + term(far + twin_of)
-    arrive(lo(far_p), 8)
-    arrive(hi(far_p), 9)
-    push(wbuf.at[far_p], 17, twin, mine)
+    for load in loads[4:]:
+        load.wait()
+    spread[...], gather[...] = dispatch_tables(
+        own_ref[...].astype(F32), mask_ref[...].astype(F32)
+    )
+
+    def to_slabs(rows):
+        return rows.reshape(rows.shape[0] // SLAB, SLAB, rows.shape[1]).astype(BF16)
+
+    hid_out[...] = to_slabs(dot(spread[...], hid_ref[...]))
+    arrive(wbuf.at[left_p + twin_of], 19)
+    arrive(wbuf.at[right_p + twin_of], 20)
+    acc[...] += term(left_p + twin_of) + term(right_p + twin_of)
+    arrive(lo(far_p), 12)
+    push(lo(far_p), 21, twin, mine)
+    arrive(hi(far_p), 13)
+    push(hi(far_p), 22, twin, mine)
     acc[...] += term(far_p)
-    arrive(wbuf.at[left_p + twin_of], 15)
-    arrive(wbuf.at[right_p + twin_of], 16)
-    acc[...] += term(left_p + twin_of) + term(right_p + twin_of)
-    arrive(wbuf.at[far_p + twin_of], 17)
+    arrive(lo(far_p + twin_of), 21)
+    arrive(hi(far_p + twin_of), 22)
     acc[...] += term(far_p + twin_of)
 
     def head_place(h):
@@ -313,35 +362,86 @@
         def _():
             pltpu.make_async_copy(head_out.at[h], head_in.at[me], head_recv.at[me]).start()
 
-    def exchange(out, into, send, recv):
-        @pl.loop(1, GRP)
+    def outward(way, n):
+        out, into, send, recv = way
+        m = n // 4
+        dz = GRP // 8 + (m + 1) // 2 * (1 - 2 * lax.rem(m, 2))
+        to = lax.rem(z + dz, GRP // 4) * 4 + lax.rem(n, 4)
+        slot = (GRP // 4 - dz) * 4 + yh
+        pltpu.make_async_remote_copy(
+            src_ref=out.at[to],
+            dst_ref=into.at[slot],
+            send_sem=send.at[n],
+            recv_sem=recv.at[slot],
+            device_id={"seq": me, "grp": to},
+        ).start()
+
+    def outward_near(way):
+        out, into, send, recv = way
+
+        @pl.loop(1, 4)
         def _(k):
-            to = lax.rem(mine + k, GRP)
+            to = z * 4 + lax.rem(yh + k, 4)
             pltpu.make_async_remote_copy(
                 src_ref=out.at[to],
-                dst_ref=into.at[mine],
-                send_sem=send.at[to],
-                recv_sem=recv.at[mine],
+                dst_ref=into.at[yh],
+                send_sem=send.at[GRP - 5 + k],
+                recv_sem=recv.at[yh],
                 device_id={"seq": me, "grp": to},
             ).start()
 
-        pltpu.make_async_copy(out.at[mine], into.at[mine], recv.at[mine]).start()
-
-    def received(out, into, send, recv):
-        @pl.loop(0, GRP)
+        pltpu.make_async_copy(out.at[mine], into.at[yh], recv.at[yh]).start()
+
+    def exchange(way):
+        @pl.loop(0, GRP - 4)
+        def _(n):
+            outward(way, n)
+
+        outward_near(way)
+
+    def received(way, first, last):
+        out, into, send, recv = way
+
+        @pl.loop(first, last)
         def _(k):
             pltpu.make_async_copy(out.at[k], into.at[k], recv.at[k]).wait()
 
-    def sent(out, into, send, recv):
-        @pl.loop(1, GRP)
+    def sent(way, first, last):
+        out, into, send, recv = way
+
+        @pl.loop(first, last)
         def _(k):
-            to = lax.rem(mine + k, GRP)
-            pltpu.make_async_copy(out.at[to], into.at[to], send.at[to]).wait()
+            pltpu.make_async_copy(out.at[k], into.at[k], send.at[k]).wait()
+
+    def homeward(first, last):
+        @pl.loop(first, last)
+        def _(j):
+            to = lax.rem(z + j // 4, GRP // 4) * 4 + lax.rem(j, 4)
+            pltpu.make_async_remote_copy(
+                src_ref=grad_out.at[j],
+                dst_ref=grad_in.at[mine],
+                send_sem=grad_send.at[j],
+                recv_sem=grad_recv.at[mine],
+                device_id={"seq": me, "grp": to},
+            ).start()
+
+    def homeward_near():
+        @pl.loop(1, 4)
+        def _(k):
+            j = lax.rem(yh + k, 4)
+            pltpu.make_async_remote_copy(
+                src_ref=grad_out.at[j],
+                dst_ref=grad_in.at[mine],
+                send_sem=grad_send.at[j],
+                recv_sem=grad_recv.at[mine],
+                device_id={"seq": me, "grp": z * 4 + j},
+            ).start()
+
+        pltpu.make_async_copy(grad_out.at[yh], grad_in.at[mine], grad_recv.at[mine]).start()
 
     hid_way = (hid_out, hid_in, hid_send, hid_recv)
     tgt_way = (tgt_out, tgt_in, tgt_send, tgt_recv)
     grad_way = (grad_out, grad_in, grad_send, grad_recv)
-    exchange(*hid_way)
 
     even = lax.rem(me, 2) == 0
     is_head = even | ((lax.rem(me, 4) == 1) & (me < 12))
@@ -371,6 +471,8 @@
                 parts.append(jnp.concatenate([zero, packed[:, HEAD:]], axis=1))
                 parts.append(jnp.concatenate([zero, packed[:, :HEAD]], axis=1))
             q = jnp.concatenate(parts, axis=0)
+            for j in range(5):
+                outward(hid_way, 5 * i + j)
             kv = head_in[:, :ROWS].reshape(SEQ * ROWS, 2 * HEAD)
             score = dot_t(q, kv)
             expo = jnp.exp2(score * rate).astype(BF16)
@@ -397,6 +499,16 @@
                         att_out.at[to], att_in.at[my_head], att_recv.at[my_head]
                     ).start()
 
+        @pl.loop(5 * SEQ // 2, GRP - 4)
+        def _(n):
+            outward(hid_way, n)
+
+        outward_near(hid_way)
+
+    @pl.when(jnp.logical_not(is_head))
+    def _():
+        exchange(hid_way)
+
     @pl.loop(0, HEADS)
     def _(h):
         pltpu.make_async_copy(att_out.at[0], att_in.at[h], att_recv.at[h]).wait()
@@ -404,27 +516,36 @@
     top = jnp.concatenate([att_in[h][:, :HEAD].astype(F32) for h in range(HEADS)], axis=1)
     low = jnp.concatenate([att_in[h][:, HEAD:].astype(F32) for h in range(HEADS)], axis=1)
     attended = jnp.concatenate([top, low], axis=0)
-    targets = normalize(attended)[0].astype(BF16)
-    tgt_ref[...] = targets
-    to_slabs(dot(spread[...], targets), tgt_out)
-    exchange(*tgt_way)
-
-    def from_slabs(into):
-        return into[...].reshape(SLOTS, into.shape[2])
-
-    received(*hid_way)
-    inputs = from_slabs(hid_in).astype(F32)
-    normed_h, inverse = normalize(inputs)
-    predicted[...] = dot_t(normed_h.astype(BF16), pw_ref[...])
-    received(*tgt_way)
-    residual = (predicted[...] - from_slabs(tgt_in).astype(F32)).astype(BF16)
-    upstream = dot(residual, pw_ref[...])
-    upstream_mean = jnp.mean(upstream, axis=-1, keepdims=True)
-    cross_mean = jnp.mean(upstream * normed_h, axis=-1, keepdims=True)
-    to_slabs(inverse * (upstream - upstream_mean - normed_h * cross_mean), grad_out)
-    exchange(*grad_way)
-    received(*grad_way)
-    pg_ref[...] = dot(gather[...], from_slabs(grad_in)).astype(BF16)
+    targets = normalize(attended)[0]
+    tgt_out[...] = to_slabs(dot(spread[...], targets.astype(BF16)))
+    exchange(tgt_way)
+    tgt_ref[...] = targets.T.astype(BF16)
+
+    received(hid_way, 0, GRP)
+    owned, inverse = normalize(hid_in[...].reshape(SLOTS, PRED).astype(F32))
+    normed_h[...] = owned
+    inverses[...] = inverse
+    predicted[...] = dot_t(owned.astype(BF16), pw_ref[...])
+
+    for first, last in ((16, 36), (0, 16), (36, 48)):
+        rows = slice(first * SLAB, last * SLAB)
+        received(tgt_way, first, last)
+        landed = tgt_in[first:last].reshape((last - first) * SLAB, ATT).astype(F32)
+        upstream = dot((predicted[rows] - landed).astype(BF16), pw_ref[...])
+        own = normed_h[rows]
+        upstream_mean = jnp.mean(upstream, axis=-1, keepdims=True)
+        cross_mean = jnp.mean(upstream * own, axis=-1, keepdims=True)
+        grad_out[first:last] = to_slabs(
+            inverses[rows] * (upstream - upstream_mean - own * cross_mean)
+        )
+        if first == 0:
+            homeward(4, last)
+            homeward_near()
+        else:
+            homeward(first, last)
+
+    received(grad_way, 0, GRP)
+    pg_ref[...] = dot(gather[...], grad_in[...].reshape(SLOTS, PRED)).astype(BF16)
 
     for copy in started:
         copy.wait_send()
@@ -441,9 +562,25 @@
             to = lax.rem(me + k, SEQ)
             pltpu.make_async_copy(att_out.at[to], att_in.at[0], att_send.at[to]).wait()
 
-    sent(*hid_way)
-    sent(*tgt_way)
-    sent(*grad_way)
+    sent(hid_way, 0, GRP - 1)
+    sent(tgt_way, 0, GRP - 1)
+    sent(grad_way, 4, GRP)
+
+    @pl.loop(1, 4)
+    def _(k):
+        j = lax.rem(yh + k, 4)
+        pltpu.make_async_copy(grad_out.at[j], grad_in.at[j], grad_send.at[j]).wait()
+
+
+def finish(nkv_in, tgt_in, pg_in, nkv_out, tgt_out, pg_out, sem):
+    copies = [
+        pltpu.make_async_copy(src, dst, sem.at[i])
+        for i, (src, dst) in enumerate(((tgt_in, tgt_out), (nkv_in, nkv_out), (pg_in, pg_out)))
+    ]
+    for copy in copies:
+        copy.start()
+    for copy in copies:
+        copy.wait()
 
 
 def shards(
@@ -451,16 +588,25 @@
 ):
     vmem = pl.BlockSpec(memory_space=pltpu.VMEM)
     dma = pltpu.SemaphoreType.DMA
-    new_kv, targets, pred_grad = pl.pallas_call(
+    results = pl.pallas_call(
         kernel,
         out_shape=(
             jax.ShapeDtypeStruct((SHARD, D), BF16),
-            jax.ShapeDtypeStruct((ROWS, ATT), BF16),
+            jax.ShapeDtypeStruct((ATT, ROWS), BF16),
             jax.ShapeDtypeStruct((ROWS, PRED), BF16),
         ),
-        in_specs=[vmem] * 8,
+        in_specs=[pl.BlockSpec(memory_space=pl.ANY)] * 8,
         out_specs=(vmem,) * 3,
         scratch_shapes=[
+            pltpu.VMEM((ROWS, D), BF16),
+            pltpu.VMEM((SHARD, D), BF16),
+            pltpu.VMEM((SHARD, D), BF16),
+            pltpu.VMEM((ATT, D), BF16),
+            pltpu.VMEM((ROWS, PRED), BF16),
+            pltpu.VMEM((ATT, PRED), BF16),
+            pltpu.VMEM((1, PAIRS), jnp.int32),
+            pltpu.VMEM((1, PAIRS), jnp.int32),
+            dma((8,)),
             pltpu.VMEM((SEQ, SHARD, D), BF16),
             pltpu.VMEM((SEQ, ROWS, SHARD), BF16),
             pltpu.VMEM((ROWS, D), F32),
@@ -479,8 +625,10 @@
             pltpu.VMEM((GRP, SLAB, PRED), BF16),
             pltpu.VMEM((GRP, SLAB, PRED), BF16),
             pltpu.VMEM((SLOTS, ATT), F32),
-            dma((24,)),
-            dma((18,)),
+            pltpu.VMEM((SLOTS, PRED), F32),
+            pltpu.VMEM((SLOTS, 1), F32),
+            dma((23,)),
+            dma((23,)),
             dma((HEADS,)),
             dma((SEQ,)),
             dma((SEQ,)),
@@ -493,7 +641,7 @@
             dma((GRP,)),
         ],
         compiler_params=pltpu.CompilerParams(
-            collective_id=0, has_side_effects=True, vmem_limit_bytes=48 * 1024 * 1024
+            collective_id=0, has_side_effects=True, vmem_limit_bytes=63 * 1024 * 1024
         ),
         cost_estimate=pl.CostEstimate(
             flops=2_000_000_000, bytes_accessed=5_000_000, transcendentals=3_000_000
@@ -507,9 +655,18 @@
         pred_hidden[0],
         pred_weight[0],
         target_mask,
-        owners[0],
-    )
-    return new_kv, targets[None], pred_grad[None]
+        owners[0].reshape(1, PAIRS),
+    )
+    anywhere = pl.BlockSpec(memory_space=pl.ANY)
+    new_kv, targets, pred_grad = pl.pallas_call(
+        finish,
+        out_shape=tuple(jax.ShapeDtypeStruct(r.shape, r.dtype) for r in results),
+        in_specs=[anywhere] * 3,
+        out_specs=(anywhere,) * 3,
+        scratch_shapes=[dma((3,))],
+        name="finish",
+    )(*results)
+    return new_kv, targets.T[None], pred_grad[None]
 
 
 def solution(mesh):

time: 106 us -> 106 us (level)
  the two profiles are of different devices: /device:TPU:8 before, /device:TPU:14 now
where the time goes in v2:
time: 106 us
  Pallas kernels  105 us (99%)
    pallas_call x1, Pallas kernels, shards(): pl.pallas_call(kernel, out_shape=(jax.ShapeDtypeStruct((SHARD, D), BF16),...  88 us
    pallas_call x1, Pallas kernels, shards(): pl.pallas_call(finish, out_shape=tuple((jax.ShapeDtypeStruct(r.shape, r.d...  17.1 us

profile of v2, /device:TPU:14, one launch (start us, length us, event | category | flops | bytes accessed | tf_op | source)
XLA Modules:
  0.0 105.7 jit_solution(4008449723448116618)
XLA Ops:
  0.6 88.0 %attend_and_route.1 = (bf16[88,1408]{1,0:T(8,128)(2,1)}, bf16[704,128]{1,0:T(8,128)(2,1)}, bf16[128,384]{1,0:T(8,128)(2,1)}) custom-call(bf16[128,1408]{1,0:T(8,128)(2,1)} %bitcast.9, bf16[88,1408]{1,0:T(8,128)(2,1)} %tkv_hbm.1, bf16[88,1408]{1,0:T(8,128)(2,1)} %ckv_hbm.1, bf16[704,1408]{1,0:T(8,128)(2,1)} %qw_hbm.1, bf16[128,384]{1,0:T(8,128)(2,1)} %bitcast.11, ...), custom_call_target="tpu_custom_call" | custom-call | flops 2000000000 | bytes 5000000 | tf_op jit(solution)/shard_map/attend_and_route/pallas_call | solution.py:591
  88.6 17.1 %finish.1 = (bf16[88,1408]{1,0:T(8,128)(2,1)}, bf16[704,128]{1,0:T(8,128)(2,1)}, bf16[128,384]{1,0:T(8,128)(2,1)}) custom-call(bf16[88,1408]{1,0:T(8,128)(2,1)} %get-tuple-element.9.nkv_in, bf16[704,128]{1,0:T(8,128)(2,1)} %get-tuple-element.10.tgt_in, bf16[128,384]{1,0:T(8,128)(2,1)} %get-tuple-element.11.pg_in), custom_call_target="tpu_custom_call" | custom-call | tf_op jit(solution)/shard_map/finish/pallas_call | solution.py:661

commit v3 on v2

--- a/solution.py
+++ b/solution.py
@@ -591,9 +591,9 @@
     results = pl.pallas_call(
         kernel,
         out_shape=(
-            jax.ShapeDtypeStruct((SHARD, D), BF16),
-            jax.ShapeDtypeStruct((ATT, ROWS), BF16),
-            jax.ShapeDtypeStruct((ROWS, PRED), BF16),
+            pltpu.VMEM((SHARD, D), BF16),
+            pltpu.VMEM((ATT, ROWS), BF16),
+            pltpu.VMEM((ROWS, PRED), BF16),
         ),
         in_specs=[pl.BlockSpec(memory_space=pl.ANY)] * 8,
         out_specs=(vmem,) * 3,
@@ -641,21 +641,26 @@
             dma((GRP,)),
         ],
         compiler_params=pltpu.CompilerParams(
-            collective_id=0, has_side_effects=True, vmem_limit_bytes=63 * 1024 * 1024
+            collective_id=0, has_side_effects=True, vmem_limit_bytes=56 * 1024 * 1024
         ),
         cost_estimate=pl.CostEstimate(
             flops=2_000_000_000, bytes_accessed=5_000_000, transcendentals=3_000_000
         ),
         name="attend_and_route",
     )(
-        tokens[0],
-        target_kv,
-        context_kv,
-        query_weight,
-        pred_hidden[0],
-        pred_weight[0],
-        target_mask,
-        owners[0].reshape(1, PAIRS),
+        *(
+            pltpu.with_memory_space_constraint(argument, pltpu.HBM)
+            for argument in (
+                tokens[0],
+                target_kv,
+                context_kv,
+                query_weight,
+                pred_hidden[0],
+                pred_weight[0],
+                target_mask,
+                owners[0].reshape(1, PAIRS),
+            )
+        )
     )
     anywhere = pl.BlockSpec(memory_space=pl.ANY)
     new_kv, targets, pred_grad = pl.pallas_call(
@@ -665,7 +670,7 @@
         out_specs=(anywhere,) * 3,
         scratch_shapes=[dma((3,))],
         name="finish",
-    )(*results)
+    )(*(pltpu.with_memory_space_constraint(r, pltpu.VMEM) for r in results))
     return new_kv, targets.T[None], pred_grad[None]
 
 

time: 106 us -> 88.9 us (0.84)
  Pallas kernels: 105 us -> 88.1 us
    pallas_call x1, Pallas kernels: 17.1 us -> 0.81 us  [shards(): pl.pallas_call(finish, out_shape=tuple((jax.ShapeDtypeStruct(r.shape, r.d...]
where the time goes in v3:
time: 88.9 us; the launch traced here: 88.8 us
  Pallas kernels  88.1 us (99%)
    pallas_call x1, Pallas kernels, shards(): pl.pallas_call(kernel, out_shape=(pltpu.VMEM((SHARD, D), BF16), pltpu.VME...  87.3 us

profile of v3, /device:TPU:14, one launch (start us, length us, event | category | flops | bytes accessed | tf_op | source)
XLA Modules:
  0.0 88.8 jit_solution(10442153214202101956)
XLA Ops:
  0.6 87.3 %attend_and_route.1 = (bf16[88,1408]{1,0:T(8,128)(2,1)S(1)}, bf16[704,128]{1,0:T(8,128)(2,1)S(1)}, bf16[128,384]{1,0:T(8,128)(2,1)S(1)}) custom-call(bf16[128,1408]{1,0:T(8,128)(2,1)} %bitcast.9, bf16[88,1408]{1,0:T(8,128)(2,1)} %tkv_hbm.1, bf16[88,1408]{1,0:T(8,128)(2,1)} %ckv_hbm.1, bf16[704,1408]{1,0:T(8,128)(2,1)} %qw_hbm.1, bf16[128,384]{1,0:T(8,128)(2,1)} %bitcast.11, ...), custom_call_target="tpu_custom_call" | custom-call | flops 2000000000 | bytes 5000000 | tf_op jit(solution)/shard_map/attend_and_route/pallas_call | solution.py:591
  88.0 0.8 finish.1

commit v4 on v3

--- a/solution.py
+++ b/solution.py
@@ -19,6 +19,7 @@
 SHARD = 88
 LO = 768
 SLAB = 4
+BURST = 8
 SLOTS = GRP * SLAB
 
 keep_rate = 0.9
@@ -211,6 +212,9 @@
     down_grp = z * 4 + lax.rem(yh + 3 * (1 - y), 4)
     other_grp = z * 4 + lax.rem(yh + 3 + 2 * y, 4)
 
+    def lane_of(to_yh):
+        return jnp.where(lax.rem(to_yh - yh + 4, 4) == 2, across, me)
+
     barrier = pltpu.get_barrier_semaphore()
 
     @pl.loop(1, SEQ)
@@ -219,7 +223,10 @@
 
     @pl.loop(1, GRP)
     def _(k):
-        pl.semaphore_signal(barrier, inc=1, device_id={"seq": me, "grp": lax.rem(mine + k, GRP)})
+        to = lax.rem(mine + k, GRP)
+        pl.semaphore_signal(
+            barrier, inc=1, device_id={"seq": lane_of(lax.rem(to, 4)), "grp": to}
+        )
 
     pl.semaphore_signal(barrier, inc=1, device_id={"seq": across, "grp": other_grp})
 
@@ -338,7 +345,7 @@
     acc[...] += term(far_p + twin_of)
 
     def head_place(h):
-        return 2 * h if h < 8 else 1 + 4 * (h - 8)
+        return jnp.where(h < 8, 2 * h, 4 * h - 31)
 
     for h in range(HEADS):
         k_h = acc[:, h * HEAD : (h + 1) * HEAD]
@@ -346,6 +353,10 @@
         q_h = queries[:, h * HEAD : (h + 1) * HEAD]
         head_out[h, :ROWS] = jnp.concatenate([v_h, k_h], axis=1).astype(BF16)
         head_out[h, ROWS:] = jnp.concatenate([q_h[PAIRS:], q_h[:PAIRS]], axis=1).astype(BF16)
+
+    @pl.loop(0, HEADS)
+    def _(k):
+        h = lax.rem(me + k, HEADS)
         to = head_place(h)
 
         @pl.when(me != to)
@@ -362,19 +373,22 @@
         def _():
             pltpu.make_async_copy(head_out.at[h], head_in.at[me], head_recv.at[me]).start()
 
-    def outward(way, n):
+    def outward(way):
         out, into, send, recv = way
-        m = n // 4
-        dz = GRP // 8 + (m + 1) // 2 * (1 - 2 * lax.rem(m, 2))
-        to = lax.rem(z + dz, GRP // 4) * 4 + lax.rem(n, 4)
-        slot = (GRP // 4 - dz) * 4 + yh
-        pltpu.make_async_remote_copy(
-            src_ref=out.at[to],
-            dst_ref=into.at[slot],
-            send_sem=send.at[n],
-            recv_sem=recv.at[slot],
-            device_id={"seq": me, "grp": to},
-        ).start()
+
+        @pl.loop(0, GRP // 4 - 1)
+        def _(m):
+            dz = GRP // 8 + (m + 1) // 2 * (1 - 2 * lax.rem(m, 2))
+            base = lax.rem(z + dz, GRP // 4) * 4
+            slot = (GRP // 4 - dz) * 4 + yh
+            for c in range(4):
+                pltpu.make_async_remote_copy(
+                    src_ref=out.at[base + c],
+                    dst_ref=into.at[slot],
+                    send_sem=send.at[m * 4 + c],
+                    recv_sem=recv.at[slot],
+                    device_id={"seq": lane_of(c), "grp": base + c},
+                ).start()
 
     def outward_near(way):
         out, into, send, recv = way
@@ -387,16 +401,13 @@
                 dst_ref=into.at[yh],
                 send_sem=send.at[GRP - 5 + k],
                 recv_sem=recv.at[yh],
-                device_id={"seq": me, "grp": to},
+                device_id={"seq": jnp.where(k == 2, across, me), "grp": to},
             ).start()
 
         pltpu.make_async_copy(out.at[mine], into.at[yh], recv.at[yh]).start()
 
     def exchange(way):
-        @pl.loop(0, GRP - 4)
-        def _(n):
-            outward(way, n)
-
+        outward(way)
         outward_near(way)
 
     def received(way, first, last):
@@ -414,16 +425,17 @@
             pltpu.make_async_copy(out.at[k], into.at[k], send.at[k]).wait()
 
     def homeward(first, last):
-        @pl.loop(first, last)
-        def _(j):
-            to = lax.rem(z + j // 4, GRP // 4) * 4 + lax.rem(j, 4)
-            pltpu.make_async_remote_copy(
-                src_ref=grad_out.at[j],
-                dst_ref=grad_in.at[mine],
-                send_sem=grad_send.at[j],
-                recv_sem=grad_recv.at[mine],
-                device_id={"seq": me, "grp": to},
-            ).start()
+        @pl.loop(first // 4, last // 4)
+        def _(dz):
+            base = lax.rem(z + dz, GRP // 4) * 4
+            for c in range(4):
+                pltpu.make_async_remote_copy(
+                    src_ref=grad_out.at[dz * 4 + c],
+                    dst_ref=grad_in.at[mine],
+                    send_sem=grad_send.at[dz * 4 + c],
+                    recv_sem=grad_recv.at[mine],
+                    device_id={"seq": lane_of(c), "grp": base + c},
+                ).start()
 
     def homeward_near():
         @pl.loop(1, 4)
@@ -434,7 +446,7 @@
                 dst_ref=grad_in.at[mine],
                 send_sem=grad_send.at[j],
                 recv_sem=grad_recv.at[mine],
-                device_id={"seq": me, "grp": z * 4 + j},
+                device_id={"seq": jnp.where(k == 2, across, me), "grp": z * 4 + j},
             ).start()
 
         pltpu.make_async_copy(grad_out.at[yh], grad_in.at[mine], grad_recv.at[mine]).start()
@@ -443,45 +455,47 @@
     tgt_way = (tgt_out, tgt_in, tgt_send, tgt_recv)
     grad_way = (grad_out, grad_in, grad_send, grad_recv)
 
+    exchange(hid_way)
+
     even = lax.rem(me, 2) == 0
     is_head = even | ((lax.rem(me, 4) == 1) & (me < 12))
     my_head = jnp.where(even, me // 2, 8 + me // 4)
 
     @pl.when(is_head)
     def _():
+        lane = iota((ROWS, 2 * HEAD), 1)
+
         @pl.loop(0, SEQ)
         def _(t):
             pltpu.make_async_copy(head_out.at[0], head_in.at[t], head_recv.at[t]).wait()
-
-        lane = iota((ROWS, 2 * HEAD), 1)
-
-        @pl.loop(0, SEQ)
-        def _(t):
             block = head_in[t, :ROWS].astype(F32)
             values_one[t] = jnp.where(lane < HEAD, block, 1.0).astype(BF16)
 
         rate = math.log2(math.e) / math.sqrt(HEAD)
 
-        @pl.loop(0, SEQ // 2)
+        @pl.loop(0, SEQ // BURST)
         def _(i):
             zero = jnp.zeros((PAIRS, HEAD), BF16)
             parts = []
-            for j in range(2):
-                packed = head_in[2 * i + j, ROWS:]
+            for j in range(BURST):
+                packed = head_in[BURST * i + j, ROWS:]
                 parts.append(jnp.concatenate([zero, packed[:, HEAD:]], axis=1))
                 parts.append(jnp.concatenate([zero, packed[:, :HEAD]], axis=1))
             q = jnp.concatenate(parts, axis=0)
-            for j in range(5):
-                outward(hid_way, 5 * i + j)
             kv = head_in[:, :ROWS].reshape(SEQ * ROWS, 2 * HEAD)
             score = dot_t(q, kv)
             expo = jnp.exp2(score * rate).astype(BF16)
             added = dot(expo, values_one[...].reshape(SEQ * ROWS, 2 * HEAD))
             attended = added[:, :HEAD] / added[:, HEAD:]
-            for j in range(2):
+            for j in range(BURST):
                 rows = attended[j * ROWS : (j + 1) * ROWS]
-                to = 2 * i + j
-                att_out[to] = jnp.concatenate([rows[:PAIRS], rows[PAIRS:]], axis=1).astype(BF16)
+                att_out[BURST * i + j] = jnp.concatenate(
+                    [rows[:PAIRS], rows[PAIRS:]], axis=1
+                ).astype(BF16)
+
+            @pl.loop(0, BURST)
+            def _(k):
+                to = BURST * i + lax.rem(me + k, BURST)
 
                 @pl.when(me != to)
                 def _():
@@ -498,16 +512,6 @@
                     pltpu.make_async_copy(
                         att_out.at[to], att_in.at[my_head], att_recv.at[my_head]
                     ).start()
-
-        @pl.loop(5 * SEQ // 2, GRP - 4)
-        def _(n):
-            outward(hid_way, n)
-
-        outward_near(hid_way)
-
-    @pl.when(jnp.logical_not(is_head))
-    def _():
-        exchange(hid_way)
 
     @pl.loop(0, HEADS)
     def _(h):

time: 88.9 us -> 89.7 us (level)
  the two profiles are of different devices: /device:TPU:14 before, /device:TPU:8 now
where the time goes in v4:
time: 89.7 us; the launch traced here: 89.5 us
  Pallas kernels  88.9 us (99%)
    pallas_call x1, Pallas kernels, shards(): pl.pallas_call(kernel, out_shape=(pltpu.VMEM((SHARD, D), BF16), pltpu.VME...  88.1 us

profile of v4, /device:TPU:8, one launch (start us, length us, event | category | flops | bytes accessed | tf_op | source)
XLA Modules:
  0.0 89.5 jit_solution(6266889833687457657)
XLA Ops:
  0.6 88.1 %attend_and_route.1 = (bf16[88,1408]{1,0:T(8,128)(2,1)S(1)}, bf16[704,128]{1,0:T(8,128)(2,1)S(1)}, bf16[128,384]{1,0:T(8,128)(2,1)S(1)}) custom-call(bf16[128,1408]{1,0:T(8,128)(2,1)} %bitcast.9, bf16[88,1408]{1,0:T(8,128)(2,1)} %tkv_hbm.1, bf16[88,1408]{1,0:T(8,128)(2,1)} %ckv_hbm.1, bf16[704,1408]{1,0:T(8,128)(2,1)} %qw_hbm.1, bf16[128,384]{1,0:T(8,128)(2,1)} %bitcast.11, ...), custom_call_target="tpu_custom_call" | custom-call | flops 2000000000 | bytes 5000000 | tf_op jit(solution)/shard_map/attend_and_route/pallas_call | solution.py:595
  88.7 0.8 finish.1

commit v5 on v4

--- a/solution.py
+++ b/solution.py
@@ -19,7 +19,7 @@
 SHARD = 88
 LO = 768
 SLAB = 4
-BURST = 8
+BURST = 4
 SLOTS = GRP * SLAB
 
 keep_rate = 0.9
@@ -345,7 +345,7 @@
     acc[...] += term(far_p + twin_of)
 
     def head_place(h):
-        return jnp.where(h < 8, 2 * h, 4 * h - 31)
+        return 2 * h if h < 8 else 1 + 4 * (h - 8)
 
     for h in range(HEADS):
         k_h = acc[:, h * HEAD : (h + 1) * HEAD]
@@ -353,10 +353,6 @@
         q_h = queries[:, h * HEAD : (h + 1) * HEAD]
         head_out[h, :ROWS] = jnp.concatenate([v_h, k_h], axis=1).astype(BF16)
         head_out[h, ROWS:] = jnp.concatenate([q_h[PAIRS:], q_h[:PAIRS]], axis=1).astype(BF16)
-
-    @pl.loop(0, HEADS)
-    def _(k):
-        h = lax.rem(me + k, HEADS)
         to = head_place(h)
 
         @pl.when(me != to)

time: 89.7 us -> 87.2 us (0.972)
  the two profiles are of different devices: /device:TPU:8 before, /device:TPU:14 now
where the time goes in v5:
time: 87.2 us; the launch traced here: 87.1 us
  Pallas kernels  86.4 us (99%)
    pallas_call x1, Pallas kernels, shards(): pl.pallas_call(kernel, out_shape=(pltpu.VMEM((SHARD, D), BF16), pltpu.VME...  85.6 us

profile of v5, /device:TPU:14, one launch (start us, length us, event | category | flops | bytes accessed | tf_op | source)
XLA Modules:
  0.0 87.1 jit_solution(18244836410485056599)
XLA Ops:
  0.6 85.6 %attend_and_route.1 = (bf16[88,1408]{1,0:T(8,128)(2,1)S(1)}, bf16[704,128]{1,0:T(8,128)(2,1)S(1)}, bf16[128,384]{1,0:T(8,128)(2,1)S(1)}) custom-call(bf16[128,1408]{1,0:T(8,128)(2,1)} %bitcast.9, bf16[88,1408]{1,0:T(8,128)(2,1)} %tkv_hbm.1, bf16[88,1408]{1,0:T(8,128)(2,1)} %ckv_hbm.1, bf16[704,1408]{1,0:T(8,128)(2,1)} %qw_hbm.1, bf16[128,384]{1,0:T(8,128)(2,1)} %bitcast.11, ...), custom_call_target="tpu_custom_call" | custom-call | flops 2000000000 | bytes 5000000 | tf_op jit(solution)/shard_map/attend_and_route/pallas_call | solution.py:591
  86.2 0.8 finish.1
